TPU v7x, 32 devices: a whole 2x2x4 slice. The times are simulated.
32 devices in a mesh: groups: 2 (over x), gx: 16 (over z, y, core).
Axes of the slice: x: 2, y: 2, z: 4, core: 2. Of those that a mesh axis runs over, the one named last changes fastest.
Arguments:
- snapshots: float32 [256, 192, 8, 128], P('groups', 'gx'), parts along dimension 0, may hold values from -120 to 120
- coefficient: float32 [384, 8, 128], P(('groups', 'gx')), parts along dimension 0, may hold values from 0.5 to 4
Outputs:
- factor: float32 [256, 128], P('groups'), parts along dimension 0
- image: float32 [128, 384, 8, 128], P(None, ('groups', 'gx')), parts along dimension 1
- reduced: float32 [256, 128], P('groups'), parts along dimension 0
There are 2 independent parts, one for each index of `groups`. A program takes and returns all parts, laid end to end along the dimension named above; each array names one. Nothing has to cross between parts.
All inputs are finite; a program needn't handle non-finite values.
Results may differ from a plain program's by a relative error of at most 0.00012.
Values sent between devices are 32-bit elements; how exact they have to be, the bound alone decides.
A program may use at most 128 MiB of HBM per device.

v0:
```python
import jax
import jax.numpy as jnp
from jax import lax
from jax.sharding import PartitionSpec as P

HIGH = lax.Precision.HIGHEST


def swapped(value, axis, stride):
    mask = 2**stride
    pairs = [(source, source ^ mask) for source in range(lax.axis_size(axis))]
    return lax.ppermute(value, axis, pairs)


def padded_2(block, sides, width):
    for axis, dim in sides:
        count = lax.axis_size(axis)
        forward = [(i, i + 1) for i in range(count - 1)]
        backward = [(target, source) for source, target in forward]
        low = lax.ppermute(
            lax.slice_in_dim(block, block.shape[dim] - width, None, axis=dim), axis, forward
        )
        high = lax.ppermute(lax.slice_in_dim(block, 0, width, axis=dim), axis, backward)
        block = jnp.concatenate([low, block, high], axis=dim)
    return block


def upper_of(gram):
    return jnp.linalg.cholesky(gram).T


def neighbours(padded, cx, cy, cz):
    total = jnp.zeros((padded.shape[0], cx, cy, cz), jnp.float32)
    for dx in range(3):
        for dy in range(3):
            for dz in range(3):
                if dx == 1 and dy == 1 and (dz == 1):
                    continue
                weight = 0.5 ** (abs(dx - 1) + abs(dy - 1) + abs(dz - 1))
                total = total + weight * padded[:, dx : dx + cx, dy : dy + cy, dz : dz + cz]
    return total


def stencil_apply(cube, extended, coefficient):
    kdim, cx, cy, cz = cube.shape
    padded = jnp.pad(extended, ((0, 0), (0, 0), (1, 1), (1, 1)))
    return (8.0 + coefficient) * cube - neighbours(padded, cx, cy, cz)


def shards(snapshots, coefficient):
    kdim, cx, cy, cz = snapshots.shape
    ncells = cx * lax.axis_size("gx") * cy * cz
    flat = snapshots.reshape(kdim, cx * cy * cz)
    local_gram = jnp.dot(flat, flat.T, precision=HIGH, preferred_element_type=jnp.float32) / ncells
    factor = upper_of(local_gram)
    levels = lax.axis_size("gx").bit_length() - 1
    for level in range(levels):
        partner = swapped(factor, "gx", level)
        merged = jnp.dot(
            factor.T, factor, precision=HIGH, preferred_element_type=jnp.float32
        ) + jnp.dot(partner.T, partner, precision=HIGH, preferred_element_type=jnp.float32)
        factor = upper_of(merged)
    basis = jax.scipy.linalg.solve_triangular(factor.T, flat, lower=True)
    cube = basis.reshape(kdim, cx, cy, cz)
    extended = padded_2(cube, (("gx", 1),), 1)
    image = stencil_apply(cube, extended, coefficient)
    image_flat = image.reshape(kdim, -1)
    local_reduced = (
        jnp.dot(basis, image_flat.T, precision=HIGH, preferred_element_type=jnp.float32) / ncells
    )
    reduced = lax.psum(local_reduced, "gx")
    return (factor, image, reduced)


def solution(mesh):
    placed = (P("groups", "gx", None, None), P(("groups", "gx"), None, None))
    return jax.shard_map(
        shards,
        mesh=mesh,
        in_specs=placed,
        out_specs=(P("groups", None), P(None, ("groups", "gx"), None, None), P("groups", None)),
        check_vma=False,
    )
```

profile of v0, /device:TPU:0, one launch (start us, length us, event | category | flops | bytes accessed | tf_op | source)
XLA Modules:
  0.0 401.4 jit_solution(8883873214386804952)
XLA Ops:
  7.2 0.0 all-reduce.3.cloned.1.call-start
  7.2 11.2 %fusion.45 = f32[128,128]{0,1:T(8,128)S(1)} fusion(f32[128,12,8,128]{3,2,1,0:T(8,128)} %param.3), kind=kOutput, calls=%fused_computation.77 | convolution fusion | flops 2415935488 | bytes 6356992 | tf_op jit(solution)/shard_map/dot_general | solution.py:54
  18.4 0.1 copy.8
  18.5 11.7 %cholesky.89 = f32[128,128]{1,0:T(8,128)S(1)} custom-call(f32[128,128]{1,0:T(8,128)S(1)} %fusion.53), custom_call_target="Cholesky" | custom-call | tf_op jit(solution)/shard_map/jit(cholesky)/cholesky | solution.py:29
  30.2 0.6 compare_reduce_fusion.4
  30.9 0.7 fusion.77
  31.5 0.5 collective-permute-start
  32.1 0.9 fusion.78
  33.0 0.0 collective-permute-done
  33.0 0.3 convolution_add_fusion.3
  33.2 0.1 copy.11
  33.4 11.7 %cholesky.100 = f32[128,128]{1,0:T(8,128)S(1)} custom-call(f32[128,128]{1,0:T(8,128)S(1)} %fusion.52), custom_call_target="Cholesky" | custom-call | tf_op jit(solution)/shard_map/jit(cholesky)/cholesky | solution.py:29
  45.1 0.6 compare_reduce_fusion.3
  45.8 0.7 fusion.74
  46.4 2.9 collective-permute-start.1
  49.3 0.9 fusion.75
  50.2 1.5 collective-permute-done.1
  51.8 0.3 convolution_add_fusion.2
  52.0 0.1 copy.14
  52.1 11.9 %cholesky.111 = f32[128,128]{1,0:T(8,128)S(1)} custom-call(f32[128,128]{1,0:T(8,128)S(1)} %fusion.51), custom_call_target="Cholesky" | custom-call | tf_op jit(solution)/shard_map/jit(cholesky)/cholesky | solution.py:29
  64.0 0.6 compare_reduce_fusion.2
  64.7 0.7 fusion.71
  65.3 2.0 collective-permute-start.2
  67.3 0.9 fusion.72
  68.2 1.5 collective-permute-done.2
  69.7 0.3 convolution_add_fusion.1
  69.9 0.1 copy.17
  70.1 11.7 %cholesky.122 = f32[128,128]{1,0:T(8,128)S(1)} custom-call(f32[128,128]{1,0:T(8,128)S(1)} %fusion.50), custom_call_target="Cholesky" | custom-call | tf_op jit(solution)/shard_map/jit(cholesky)/cholesky | solution.py:29
  81.8 0.6 compare_reduce_fusion.1
  82.5 0.7 fusion.68
  83.1 3.0 collective-permute-start.3
  86.1 0.9 fusion.69
  87.0 1.4 collective-permute-done.3
  88.3 0.3 convolution_add_fusion
  88.6 0.1 copy.20
  88.7 11.7 %cholesky.133 = f32[128,128]{1,0:T(8,128)S(1)} custom-call(f32[128,128]{1,0:T(8,128)S(1)} %fusion.49), custom_call_target="Cholesky" | custom-call | tf_op jit(solution)/shard_map/jit(cholesky)/cholesky | solution.py:29
  100.5 0.6 compare_reduce_fusion
  101.1 0.7 fusion.67
  101.8 9.8 %custom-call.6 = f32[1,128,128]{1,2,0:T(8,128)S(1)} custom-call(f32[1,128,128]{2,1,0:T(8,128)S(1)} %get-tuple-element.9), custom_call_target="InvertDiagBlocksLowerTriangular" | custom-call | tf_op jit(solution)/shard_map/jit(_solve_triangular)/triangular_solve | solution.py:63
  111.6 10.8 %fusion.6 = f32[128,12288]{1,0:T(8,128)S(1)} fusion(f32[16,8,96,128]{3,2,1,0:T(8,128)} %bitcast.68, f32[1,128,128]{1,2,0:T(8,128)S(1)} %custom-call.6), kind=kOutput, calls=%fused_computation.12 | convolution fusion | flops 2415919104 | bytes 12648448 | tf_op jit(solution)/shard_map/jit(_solve_triangular)/triangular_solve | solution.py:63
  122.4 0.0 copy-start.1
  122.4 0.0 copy-start.2
  122.4 1.1 copy.36
  123.5 1.5 copy-done.1
  125.0 0.0 copy-start
  125.0 0.1 fusion.101
  125.1 1.3 collective-permute-start.4
  126.4 1.3 collective-permute-start.5
  127.7 0.0 copy-done.2
  127.7 0.2 collective-permute-done.4
  127.9 4.4 %collective-permute-done.5 = f32[128,1,8,128]{3,2,1,0:T(8,128)S(1)} collective-permute-done((f32[128,1,8,128]{3,2,1,0:T(8,128)S(1)}, f32[128,1,8,128]{3,2,1,0:T(8,128)S(1)}, u32[]{:S(2)}, u32[]{:S(2)}) %collective-permute-start.5) | collective-permute-done | bytes 524320 | tf_op jit(solution)/shard_map/ppermute | solution.py:23
  132.3 0.0 copy-done
  132.3 14.4 %select_maximum_fusion = f32[128,14,10,130]{3,2,1,0:T(8,128)} fusion(f32[128,1,8,128]{3,2,1,0:T(8,128)S(1)} %collective-permute-done.5, f32[128,12,8,128]{3,2,1,0:T(8,128)S(1)} %bitcast.64, f32[128,1,8,128]{3,2,1,0:T(8,128)S(1)} %collective-permute-done.4), kind=kLoop, calls=%fused_computation.4 | loop fusion | flops 34944000 | bytes 16658432 | tf_op jit(solution)/shard_map/concatenate | solution.py:24
  146.7 139.9 %fusion.10 = f32[128,12,8,128]{3,2,1,0:T(8,128)} fusion(f32[128,14,10,130]{3,2,1,0:T(8,128)} %select_maximum_fusion, f32[128,1,8,128]{3,2,1,0:T(8,128)S(1)} %collective-permute-done.5, f32[128,12,8,128]{3,2,1,0:T(8,128)} %bitcast.65, f32[128,1,8,128]{3,2,1,0:T(8,128)S(1)} %collective-permute-done.4, f32[12,8,128]{2,1,0:T(8,128)S(1)} %broadcast_add_fusion), kind=kLoop, calls=%fused_computation.17 | loop fusion | flops 86507520 | bytes 164675584 | tf_op jit(solution)/shard_map/sub | solution.py:47
  286.5 11.1 %fusion.42 = f32[128,128]{0,1:T(8,128)} fusion(f32[128,12288]{1,0:T(8,128)} %copy-done.1, f32[16,8,96,128]{3,2,1,0:T(8,128)} %bitcast.67), kind=kOutput, calls=%fused_computation.72 | convolution fusion | flops 2415935488 | bytes 12648448 | tf_op jit(solution)/shard_map/dot_general | solution.py:69
  297.6 0.0 all-reduce.3.cloned.1.call-update
  297.6 0.7 copy.22
  298.4 94.4 %all-reduce.3.cloned.1.call-done = f32[128,128]{0,1:T(8,128)} async-done(((f32[128,128]{0,1:T(8,128)}), f32[128,128]{0,1:T(8,128)}) %all-reduce.3.cloned.1.call-update) | async-done | bytes 65552 | tf_op jit(solution)/shard_map/psum | solution.py:71
  392.8 1.6 copy.23
  (11 shorter events, 0.2 us)
Async XLA Ops:
  7.2 385.6 %all-reduce.3.cloned.1.call-start = ((), (), s32[]{:S(2)}) async-start(), calls=%async_computation | async-start | bytes 131072 | tf_op jit(solution)/shard_map/psum | solution.py:71
  31.5 1.4 collective-permute-start
  46.4 5.3 %collective-permute-start.1 = (f32[128,128]{0,1:T(8,128)S(1)}, f32[128,128]{0,1:T(8,128)S(1)}, u32[]{:S(2)}, u32[]{:S(2)}) collective-permute-start(f32[128,128]{0,1:T(8,128)S(1)} %fusion.74), channel_id=1, source_target_pairs={{0,2},{1,3},{2,0},{3,1},{4,6},{5,7},{6,4},{7,5},{8,10},{9,11},{10,... | collective-permute-start | bytes 196616 | tf_op jit(solution)/shard_map/ppermute | solution.py:12
  65.3 4.3 %collective-permute-start.2 = (f32[128,128]{0,1:T(8,128)S(1)}, f32[128,128]{0,1:T(8,128)S(1)}, u32[]{:S(2)}, u32[]{:S(2)}) collective-permute-start(f32[128,128]{0,1:T(8,128)S(1)} %fusion.71), channel_id=1, source_target_pairs={{0,4},{1,5},{2,6},{3,7},{4,0},{5,1},{6,2},{7,3},{8,12},{9,13},{10,... | collective-permute-start | bytes 196616 | tf_op jit(solution)/shard_map/ppermute | solution.py:12
  83.1 5.2 %collective-permute-start.3 = (f32[128,128]{0,1:T(8,128)S(1)}, f32[128,128]{0,1:T(8,128)S(1)}, u32[]{:S(2)}, u32[]{:S(2)}) collective-permute-start(f32[128,128]{0,1:T(8,128)S(1)} %fusion.68), channel_id=1, source_target_pairs={{0,8},{1,9},{2,10},{3,11},{4,12},{5,13},{6,14},{7,15},{8,0},{9,1},... | collective-permute-start | bytes 196616 | tf_op jit(solution)/shard_map/ppermute | solution.py:12
  122.4 2.6 copy-start.1
  122.4 5.3 %copy-start.2 = (f32[12,8,128]{2,1,0:T(8,128)S(1)}, f32[12,8,128]{2,1,0:T(8,128)}, u32[]{:S(2)}) copy-start(f32[12,8,128]{2,1,0:T(8,128)} %param.4) | copy-start | bytes 147460
  125.0 7.2 %copy-start = (f32[16,8,96,128]{3,2,1,0:T(8,128)}, f32[16,8,96,128]{3,2,1,0:T(8,128)S(1)}, u32[]{:S(2)}) copy-start(f32[16,8,96,128]{3,2,1,0:T(8,128)S(1)} %copy.36) | copy-start | bytes 18874372
  125.1 2.8 collective-permute-start.4
  126.4 5.8 %collective-permute-start.5 = (f32[128,1,8,128]{3,2,1,0:T(8,128)S(1)}, f32[128,1,8,128]{3,2,1,0:T(8,128)S(1)}, u32[]{:S(2)}, u32[]{:S(2)}) collective-permute-start(f32[128,1,8,128]{3,2,1,0:T(8,128)S(1)} %get-tuple-element.8), channel_id=1, source_target_pairs={{1,0},{2,1},{3,2},{4,3},{5,4},{6,5},{7,6},{8,7},{9,8},{10,9},{11,1... | collective-permute-start | bytes 1572872 | tf_op jit(solution)/shard_map/ppermute | solution.py:23
Sparse Core Ops, SparseCore 0:
  297.7 94.9 all-reduce.2
where the time goes:
time: 405 us; the launch traced here: 401 us
  other arithmetic  230 us (57%)
  waiting for transfers between devices  103 us (25%)
  matrix products  37.7 us (9%)
  between operations  14.5 us (4%)
  starting transfers between devices  11 us (3%)
  local copies, waits for them, and re-layouts  5.44 us (1%)
    sub x1, other arithmetic, stencil_apply(): return (8.0 + coefficient) * cube - neighbours(padded, cx, cy, cz)  140 us
    psum x1, waiting for transfers between devices, shards(): reduced = lax.psum(local_reduced, 'gx')  94.4 us
    another operation x15, other arithmetic, upper_of(): return jnp.linalg.cholesky(gram).T  62.1 us
    concatenate x1, other arithmetic, padded_2(): block = jnp.concatenate([low, block, high], axis=dim)  14.4 us
    dot_general x1, matrix products, shards(): jnp.dot(flat, flat.T, precision=HIGH, preferred_element_type=jnp.float32)  11.2 us
    dot_general x1, matrix products, shards(): jnp.dot(basis, image_flat.T, precision=HIGH, preferred_element_type=jnp.f...  11.1 us
    another operation x1, matrix products, shards(): basis = jax.scipy.linalg.solve_triangular(factor.T, flat, lower=True)  10.8 us
    another operation x2, other arithmetic, shards(): basis = jax.scipy.linalg.solve_triangular(factor.T, flat, lower=True)  10.5 us
  transfers between devices with their start and end apart: 7, of which 6 were waited for; matrix products, arithmetic and copies ran while one was open for 1% of the time, Pallas kernels for 0%

commit v1 on v0

v1 whole, which is shorter than its diff:
```python
import functools

import jax
import jax.numpy as jnp
from jax import lax
from jax.experimental import pallas as pl
from jax.experimental.pallas import tpu as pltpu
from jax.sharding import PartitionSpec as P

MESH = pl.DeviceIdType.MESH
HIGH = lax.Precision.HIGHEST
F32, BF16 = jnp.float32, jnp.bfloat16
NT = (((1,), (1,)), ((), ()))
VMEM_BYTES = 48 * 2**20


def parts_of(value):
    high = value.astype(BF16)
    return high, (value - high.astype(F32)).astype(BF16)


def sweep(low, high, body, short):
    if short:
        for i in range(low, high):
            body(i)
    else:
        lax.fori_loop(low, high, lambda i, c: (body(i), c)[1], 0)


class Sum:
    def __init__(self, n, owners, terms, slots, total, sems):
        self.n, self.owners, self.every = n, owners, n // owners
        self.terms, self.slots, self.total = terms, slots, total
        self.send1, self.recv1, self.send2, self.recv2 = sems
        self.me = lax.axis_index("gx")
        self.own = self.me // self.every
        self.short = n <= 16

    def if_owner(self, device, body):
        if self.every == 1:
            body()
        else:
            pl.when(lax.rem(device, self.every) == 0)(body)

    def first(self, d):
        dest = lax.rem(self.me + d, self.n)
        return dest, pltpu.make_async_remote_copy(
            src_ref=self.terms.at[dest // self.every],
            dst_ref=self.slots.at[d],
            send_sem=self.send1.at[d],
            recv_sem=self.recv1.at[d],
            device_id={"gx": dest},
            device_id_type=MESH,
        )

    def second(self, d):
        dest = lax.rem(self.me + d, self.n)
        return pltpu.make_async_remote_copy(
            src_ref=self.total.at[self.own],
            dst_ref=self.total.at[self.own],
            send_sem=self.send2.at[d],
            recv_sem=self.recv2.at[self.own],
            device_id={"gx": dest},
            device_id_type=MESH,
        )

    def scatter(self):
        def go(d):
            dest, copy = self.first(d)
            self.if_owner(dest, copy.start)

        sweep(1, self.n, go, self.short)

    def spread(self):
        def add():
            sweep(1, self.n, lambda d: self.first(d)[1].wait_recv(), self.short)
            value = self.terms[self.own]
            if self.short:
                for d in range(1, self.n):
                    value = value + self.slots[d]
            else:
                value = lax.fori_loop(1, self.n, lambda d, v: v + self.slots[d], value)
            self.total[self.own] = value
            sweep(1, self.n, lambda d: self.second(d).start(), self.short)

        self.if_owner(self.me, add)

    def finish(self):
        def arrived(d):
            owner = lax.rem(self.own + d, self.owners)

            def wait():
                pltpu.make_async_remote_copy(
                    src_ref=self.total.at[owner],
                    dst_ref=self.total.at[owner],
                    send_sem=self.send2.at[0],
                    recv_sem=self.recv2.at[owner],
                    device_id={"gx": lax.rem(self.me + 1, self.n)},
                    device_id_type=MESH,
                ).wait_recv()

            if self.every == 1 and d == 0:
                return
            if d == 0:
                pl.when(lax.rem(self.me, self.every) != 0)(wait)
            else:
                wait()

        for d in range(self.owners):
            arrived(d)

        def sent(d):
            dest, copy = self.first(d)
            self.if_owner(dest, copy.wait_send)

        sweep(1, self.n, sent, self.short)
        self.if_owner(
            self.me, lambda: sweep(1, self.n, lambda d: self.second(d).wait_send(), self.short)
        )


def eliminate(rest, panels, start):
    done = []
    for panel in range(start, start + panels):
        rows, width = rest.shape
        lane = lax.broadcasted_iota(jnp.int32, (1, width), 1)
        row = lax.broadcasted_iota(jnp.int32, (rows, 1), 0)
        for j in range(8):
            at = panel * 8 + j
            here = lane == at
            column = rest[:, at : at + 1]
            pivot_row = rest[j : j + 1, :]
            scaled = jnp.where(here, 1.0, pivot_row) * (1.0 / column[j : j + 1, :])
            below = row > j
            column = jnp.where(below, column, 0.0)
            rest = jnp.where(jnp.logical_and(here, below), 0.0, rest) - column * scaled
        done.append(rest[:8])
        rest = rest[8:]
    return done, rest


def reduce_kernel(
    n, owners, snap, coef, packed, hsum, applied,
    s2, sb, ab, gt, gs, gtot, ht, hs, htot,
    load_sem, halo_send, halo_recv, out_sem,
    g0, g1, g2, g3, h0, h1, h2, h3,
):
    me = lax.axis_index("gx")
    cx, cy = s2.shape[0] - 2, s2.shape[1]
    kdim, cz = s2.shape[2], s2.shape[3]
    gram = Sum(n, owners, gt, gs, gtot, (g0, g1, g2, g3))
    hess = Sum(n, owners, ht, hs, htot, (h0, h1, h2, h3))

    barrier = pltpu.get_barrier_semaphore()

    def greet(d):
        pl.semaphore_signal(
            barrier, inc=1, device_id={"gx": lax.rem(me + d, n)}, device_id_type=MESH
        )

    sweep(1, n, greet, n <= 16)

    def load(x, y):
        return pltpu.make_async_copy(
            snap.at[:, x * cy + y, 0, :], s2.at[x + 1, y], load_sem.at[x, y]
        )

    def load_plane(i, c):
        for y in range(cy):
            load(lax.rem(i + cx - 1, cx), y).start()
        return c

    lax.fori_loop(0, cx, load_plane, 0)
    pl.semaphore_wait(barrier, n - 1)

    to_right = pltpu.make_async_remote_copy(
        src_ref=s2.at[cx], dst_ref=s2.at[0], send_sem=halo_send.at[0], recv_sem=halo_recv.at[0],
        device_id={"gx": lax.rem(me + 1, n)}, device_id_type=MESH,
    )
    to_left = pltpu.make_async_remote_copy(
        src_ref=s2.at[1], dst_ref=s2.at[cx + 1], send_sem=halo_send.at[1], recv_sem=halo_recv.at[1],
        device_id={"gx": lax.rem(me + n - 1, n)}, device_id_type=MESH,
    )

    def gram_plane(x):
        for y in range(cy):
            load(x, y).wait()
        if isinstance(x, int) and x == cx - 1:
            pl.when(me < n - 1)(to_right.start)
        if isinstance(x, int) and x == 0:
            pl.when(me > 0)(to_left.start)
        for y in range(cy):
            high, low = parts_of(s2[x + 1, y])
            sb[x, 0:kdim, y * cz : (y + 1) * cz] = high
            sb[x, kdim : 2 * kdim, y * cz : (y + 1) * cz] = low
        return lax.dot_general(sb[x], sb[x, 0:kdim], NT, preferred_element_type=F32)

    total = gram_plane(cx - 1) + gram_plane(0)
    total = lax.fori_loop(1, cx - 1, lambda x, t: t + gram_plane(x), total)
    cross = total[kdim:]
    gt[...] = (total[:kdim] + (cross + cross.T)).reshape(gt.shape)
    gram.scatter()

    lane = lax.broadcasted_iota(jnp.int32, (1, 1, cz), 2)
    from_low = jnp.where(lane == 0, 0.0, 0.5)
    from_high = jnp.where(lane == cz - 1, 0.0, 0.5)
    step = 16

    def stencil_plane(x):
        diag = 9.0 + coef[x]

        def rows(b, c):
            ks = pl.ds(pl.multiple_of(b * step, step), step)
            middle = s2[x + 1, :, ks, :]
            g = middle + 0.5 * (s2[x, :, ks, :] + s2[x + 2, :, ks, :])
            for y in range(cy):
                v = g[y]
                if y == 0:
                    v = v + 0.5 * g[1]
                elif y == cy - 1:
                    v = v + 0.5 * g[cy - 2]
                else:
                    v = v + 0.5 * (g[y - 1] + g[y + 1])
                v = (
                    v
                    + from_low[0] * pltpu.roll(v, 1, 1)
                    + from_high[0] * pltpu.roll(v, cz - 1, 1)
                )
                high, low = parts_of(diag[y : y + 1, :] * middle[y] - v)
                ab[x, ks, y * cz : (y + 1) * cz] = high
                ab[x, pl.ds(pl.multiple_of(kdim + b * step, step), step), y * cz : (y + 1) * cz] = low
            return c

        lax.fori_loop(0, kdim // step, rows, 0)
        pltpu.make_async_copy(ab.at[x], applied.at[x], out_sem.at[x]).start()
        return lax.dot_general(
            sb[x], ab[x, 0:kdim], NT, preferred_element_type=F32
        ), lax.dot_general(sb[x, 0:kdim], ab[x, kdim : 2 * kdim], NT, preferred_element_type=F32)

    def stencil_sum(x, t):
        a, b = stencil_plane(x)
        return t[0] + a, t[1] + b

    zero = (jnp.zeros((2 * kdim, kdim), F32), jnp.zeros((kdim, kdim), F32))
    half = cx // 2
    t = lax.fori_loop(1, half, stencil_sum, zero)
    gram.spread()
    t = lax.fori_loop(half, cx - 1, stencil_sum, t)

    @pl.when(me > 0)
    def _():
        to_right.wait_recv()

    @pl.when(me == 0)
    def _():
        s2[0] = jnp.zeros(s2.shape[1:], F32)

    t = stencil_sum(0, t)

    @pl.when(me < n - 1)
    def _():
        to_left.wait_recv()

    @pl.when(me == n - 1)
    def _():
        s2[cx + 1] = jnp.zeros(s2.shape[1:], F32)

    t = stencil_sum(cx - 1, t)
    ht[...] = (t[0][:kdim] + t[0][kdim:] + t[1]).reshape(ht.shape)
    hess.scatter()

    gram.finish()
    ncells = cx * n * cy * cz
    rest = gtot[...].reshape(kdim, kdim) * (1.0 / ncells)
    panels = kdim // 8
    done, rest = eliminate(rest, panels // 2, 0)
    hess.spread()
    more, rest = eliminate(rest, panels - panels // 2, panels // 2)
    packed[...] = jnp.concatenate(done + more, axis=0)
    hess.finish()
    hsum[...] = htot[...].reshape(kdim, kdim) * (1.0 / ncells)

    pl.when(me < n - 1)(to_right.wait_send)
    pl.when(me > 0)(to_left.wait_send)

    def written(x, c):
        pltpu.make_async_copy(ab.at[x], applied.at[x], out_sem.at[x]).wait()
        return c

    lax.fori_loop(0, cx, written, 0)


def image_kernel(packed, hsum, applied, factor, image, reduced, ab, buf, load_sem, out_sem):
    cx, cy, kdim, cz = buf.shape

    def load(x):
        return pltpu.make_async_copy(applied.at[x], ab.at[x], load_sem.at[x])

    def start(x, c):
        load(x).start()
        return c

    lax.fori_loop(0, cx, start, 0)
    a = packed[...]
    row = lax.broadcasted_iota(jnp.int32, (kdim, kdim), 0)
    col = lax.broadcasted_iota(jnp.int32, (kdim, kdim), 1)
    pivots = jnp.sum(jnp.where(row == col, a, 0.0), axis=1, keepdims=True)
    scale = 1.0 / jnp.sqrt(pivots)
    factor[...] = jnp.where(col >= row, a * scale, 0.0)
    inverse = jnp.where(col < row, a, jnp.where(row == col, 1.0, 0.0)) * scale
    high, low = parts_of(inverse)
    twice = jnp.concatenate([high, high], axis=1)

    def store(x, y):
        return pltpu.make_async_copy(
            buf.at[x, y], image.at[:, x * cy + y, 0, :], out_sem.at[x, y]
        )

    def plane(x, c):
        load(x).wait()
        for y in range(0, cy, 2):
            at = slice(y * cz, (y + 2) * cz)
            value = jnp.dot(twice, ab[x, :, at], preferred_element_type=F32) + jnp.dot(
                low, ab[x, 0:kdim, at], preferred_element_type=F32
            )
            buf[x, y] = value[:, :cz]
            buf[x, y + 1] = value[:, cz:]
            store(x, y).start()
            store(x, y + 1).start()
        return c

    lax.fori_loop(0, cx, plane, 0)
    left = jnp.dot(inverse, hsum[...], precision=HIGH, preferred_element_type=F32)
    reduced[...] = lax.dot_general(left, inverse, NT, precision=HIGH, preferred_element_type=F32)

    def finish(x, c):
        for y in range(cy):
            store(x, y).wait()
        return c

    lax.fori_loop(0, cx, finish, 0)


def shards(n, snapshots, coefficient):
    kdim, cx, cy, cz = snapshots.shape
    owners = min(n, kdim // 8)
    rows = kdim // owners
    vmem = pl.BlockSpec(memory_space=pltpu.VMEM)
    hbm = pl.BlockSpec(memory_space=pl.ANY)
    square = jax.ShapeDtypeStruct((kdim, kdim), F32)
    dma = pltpu.SemaphoreType.DMA
    summed = [
        pltpu.VMEM((owners, rows, kdim), F32),
        pltpu.VMEM((n, rows, kdim), F32),
        pltpu.VMEM((owners, rows, kdim), F32),
    ]
    sum_sems = [dma((n,)), dma((n,)), dma((n,)), dma((owners,))]
    packed, hsum, applied = pl.pallas_call(
        functools.partial(reduce_kernel, n, owners),
        out_shape=(square, square, jax.ShapeDtypeStruct((cx, 2 * kdim, cy * cz), BF16)),
        in_specs=[hbm, vmem],
        out_specs=(vmem, vmem, hbm),
        scratch_shapes=[
            pltpu.VMEM((cx + 2, cy, kdim, cz), F32),
            pltpu.VMEM((cx, 2 * kdim, cy * cz), BF16),
            pltpu.VMEM((cx, 2 * kdim, cy * cz), BF16),
            *summed,
            *summed,
            dma((cx, cy)), dma((2,)), dma((2,)), dma((cx,)),
            *sum_sems,
            *sum_sems,
        ],
        compiler_params=pltpu.CompilerParams(
            collective_id=0, has_side_effects=True, vmem_limit_bytes=VMEM_BYTES
        ),
        name="reduce_kernel",
    )(snapshots.reshape(kdim, cx * cy, 1, cz), coefficient)
    factor, image, reduced = pl.pallas_call(
        image_kernel,
        out_shape=(square, jax.ShapeDtypeStruct((kdim, cx * cy, 1, cz), F32), square),
        in_specs=[vmem, vmem, hbm],
        out_specs=(vmem, hbm, vmem),
        scratch_shapes=[
            pltpu.VMEM((cx, 2 * kdim, cy * cz), BF16),
            pltpu.VMEM((cx, cy, kdim, cz), F32),
            dma((cx,)), dma((cx, cy)),
        ],
        compiler_params=pltpu.CompilerParams(vmem_limit_bytes=VMEM_BYTES),
        name="image_kernel",
    )(packed, hsum, applied)
    return factor, image.reshape(kdim, cx, cy, cz), reduced


def solution(mesh):
    placed = (P("groups", "gx", None, None), P(("groups", "gx"), None, None))
    return jax.shard_map(
        functools.partial(shards, mesh.shape["gx"]),
        mesh=mesh,
        in_specs=placed,
        out_specs=(P("groups", None), P(None, ("groups", "gx"), None, None), P("groups", None)),
        check_vma=False,
    )
```

time: 405 us -> 53.5 us (0.13)
  other arithmetic: 230 us -> 0 us
  waiting for transfers between devices: 103 us -> 0 us
  Pallas kernels: 0 us -> 51.9 us
  matrix products: 37.7 us -> 0 us
  between operations: 14.5 us -> 0.65 us
  starting transfers between devices: 11 us -> 0 us
  local copies, waits for them, and re-layouts: 5.44 us -> 0.79 us
    sub x1 -> x0, other arithmetic: 140 us -> none  [stencil_apply(): return (8.0 + coefficient) * cube - neighbours(padded, cx, cy, cz)]
    psum x1 -> x0, waiting for transfers between devices: 94.4 us -> none  [shards(): reduced = lax.psum(local_reduced, 'gx')]
    another operation x17 -> x0, other arithmetic: 72.5 us -> none  [the longest x15 62.1 us: upper_of(): return jnp.linalg.cholesky(gram).T]
    pallas_call x0 -> x2, Pallas kernels: none -> 51.9 us  [the longest x1 45 us: shards(): pl.pallas_call(functools.partial(reduce_kernel, n, owners), out_shape=(sq...]
    dot_general x10 -> x0, matrix products: 26.9 us -> none  [the longest x1 11.2 us: shards(): jnp.dot(flat, flat.T, precision=HIGH, preferred_element_type=jnp.float32)]
    concatenate x1 -> x0, other arithmetic: 14.4 us -> none  [padded_2(): block = jnp.concatenate([low, block, high], axis=dim)]
    ppermute x6 -> x0, starting transfers between devices: 11 us -> none  [the longest x4 8.35 us: swapped(): return lax.ppermute(value, axis, pairs)]
    another operation x1 -> x0, matrix products: 10.8 us -> none  [shards(): basis = jax.scipy.linalg.solve_triangular(factor.T, flat, lower=True)]
  transfers between devices with their start and end apart: 7 -> 0, of which waited for: 6 -> 0; matrix products, arithmetic and copies ran while one was open for 1% -> 0% of each run, Pallas kernels for 0% -> 0%
where the time goes in v1:
time: 53.5 us; the launch traced here: 53.4 us
  Pallas kernels  51.9 us (97%)
  local copies, waits for them, and re-layouts  0.79 us (1%)
  between operations  0.65 us (1%)
    pallas_call x1, Pallas kernels, shards(): pl.pallas_call(functools.partial(reduce_kernel, n, owners), out_shape=(sq...  45 us
    pallas_call x1, Pallas kernels, shards(): pl.pallas_call(image_kernel, out_shape=(square, jax.ShapeDtypeStruct((kdi...  6.92 us

profile of v1, /device:TPU:0, one launch (start us, length us, event | category | flops | bytes accessed | tf_op | source)
XLA Modules:
  0.0 53.4 jit_solution(3265660613824270642)
XLA Ops:
  0.6 0.0 copy-start
  0.6 0.8 %copy-done = f32[12,8,128]{2,1,0:T(8,128)S(1)} copy-done((f32[12,8,128]{2,1,0:T(8,128)S(1)}, f32[12,8,128]{2,1,0:T(8,128)}, u32[]{:S(2)}) %copy-start) | copy-done | bytes 49176
  1.4 45.0 %reduce_kernel.1 = (f32[128,128]{1,0:T(8,128)S(1)}, f32[128,128]{1,0:T(8,128)S(1)}, bf16[12,256,1024]{2,1,0:T(8,128)(2,1)}) custom-call(f32[128,96,1,128]{3,2,1,0:T(1,128)} %bitcast.2, f32[12,8,128]{2,1,0:T(8,128)S(1)} %copy-done), custom_call_target="tpu_custom_call" | custom-call | tf_op jit(solution)/shard_map/reduce_kernel/pallas_call | solution.py:358
  46.4 6.9 %image_kernel.1 = (f32[128,128]{1,0:T(8,128)}, f32[128,96,1,128]{3,2,1,0:T(1,128)}, f32[128,128]{1,0:T(8,128)}) custom-call(f32[128,128]{1,0:T(8,128)S(1)} %get-tuple-element.9.packed, f32[128,128]{1,0:T(8,128)S(1)} %get-tuple-element.10.hsum, bf16[12,256,1024]{2,1,0:T(8,128)(2,1)} %get-tuple-element.11.applied), custom_call_target="tpu_custom_call" | custom-call | tf_op jit(solution)/shard_map/image_kernel/pallas_call | solution.py:378
Async XLA Ops:
  0.6 0.8 %copy-start = (f32[12,8,128]{2,1,0:T(8,128)S(1)}, f32[12,8,128]{2,1,0:T(8,128)}, u32[]{:S(2)}) copy-start(f32[12,8,128]{2,1,0:T(8,128)} %coef.1) | copy-start | bytes 147460

commit v2 on v1

--- a/solution.py
+++ b/solution.py
@@ -121,27 +121,37 @@
 
 def eliminate(rest, panels, start):
     done = []
+    width = rest.shape[1]
+    lane = lax.broadcasted_iota(jnp.int32, (1, width), 1)
+    row = lax.broadcasted_iota(jnp.int32, (8, 1), 0)
     for panel in range(start, start + panels):
-        rows, width = rest.shape
-        lane = lax.broadcasted_iota(jnp.int32, (1, width), 1)
-        row = lax.broadcasted_iota(jnp.int32, (rows, 1), 0)
-        for j in range(8):
+        head, tail = rest[:8], rest[8:]
+        for j in range(0, 8, 2):
             at = panel * 8 + j
-            here = lane == at
-            column = rest[:, at : at + 1]
-            pivot_row = rest[j : j + 1, :]
-            scaled = jnp.where(here, 1.0, pivot_row) * (1.0 / column[j : j + 1, :])
-            below = row > j
-            column = jnp.where(below, column, 0.0)
-            rest = jnp.where(jnp.logical_and(here, below), 0.0, rest) - column * scaled
-        done.append(rest[:8])
-        rest = rest[8:]
+            one, two = lane == at, lane == at + 1
+            either = jnp.logical_or(one, two)
+            first, second = head[j : j + 1], head[j + 1 : j + 2]
+            c1, c2 = head[:, at : at + 1], head[:, at + 1 : at + 2]
+            p11, p12, p22 = c1[j : j + 1], c2[j : j + 1], c2[j + 1 : j + 2]
+            inverse = 1.0 / (p11 * p22 - p12 * p12)
+            row1 = jnp.where(one, 1.0, jnp.where(two, 0.0, first))
+            row2 = jnp.where(two, 1.0, jnp.where(one, 0.0, second))
+            q1 = (p22 * row1 - p12 * row2) * inverse
+            q2 = (p11 * row2 - p12 * row1) * inverse
+            if panel * 8 + 8 < width:
+                t1, t2 = tail[:, at : at + 1], tail[:, at + 1 : at + 2]
+                tail = jnp.where(either, 0.0, tail) - (t1 * q1 + t2 * q2)
+            pair = jnp.where(one, 0.0, second) - (p12 / p11) * jnp.where(one, 1.0, first)
+            lower = jnp.where(either, 0.0, head) - (c1 * q1 + c2 * q2)
+            head = jnp.where(row > j + 1, lower, jnp.where(row == j + 1, pair, head))
+        done.append(head)
+        rest = tail
     return done, rest
 
 
 def reduce_kernel(
     n, owners, snap, coef, packed, hsum, applied,
-    s2, sb, ab, gt, gs, gtot, ht, hs, htot,
+    s2, sb, ab, hacc, hlow, gt, gs, gtot, ht, hs, htot,
     load_sem, halo_send, halo_recv, out_sem,
     g0, g1, g2, g3, h0, h1, h2, h3,
 ):
@@ -205,11 +215,19 @@
     from_low = jnp.where(lane == 0, 0.0, 0.5)
     from_high = jnp.where(lane == cz - 1, 0.0, 0.5)
     step = 16
-
-    def stencil_plane(x):
+    groups = kdim // step // (cy // 2)
+
+    def stencil_plane(x, before):
         diag = 9.0 + coef[x]
 
-        def rows(b, c):
+        def chunk(b, c):
+            if before is not None:
+                products(before, b)
+            for part in range(groups):
+                rows(b * groups + part)
+            return c
+
+        def rows(b):
             ks = pl.ds(pl.multiple_of(b * step, step), step)
             middle = s2[x + 1, :, ks, :]
             g = middle + 0.5 * (s2[x, :, ks, :] + s2[x + 2, :, ks, :])
@@ -229,23 +247,34 @@
                 high, low = parts_of(diag[y : y + 1, :] * middle[y] - v)
                 ab[x, ks, y * cz : (y + 1) * cz] = high
                 ab[x, pl.ds(pl.multiple_of(kdim + b * step, step), step), y * cz : (y + 1) * cz] = low
-            return c
-
-        lax.fori_loop(0, kdim // step, rows, 0)
+
+        lax.fori_loop(0, cy // 2, chunk, 0)
         pltpu.make_async_copy(ab.at[x], applied.at[x], out_sem.at[x]).start()
-        return lax.dot_general(
-            sb[x], ab[x, 0:kdim], NT, preferred_element_type=F32
-        ), lax.dot_general(sb[x, 0:kdim], ab[x, kdim : 2 * kdim], NT, preferred_element_type=F32)
-
-    def stencil_sum(x, t):
-        a, b = stencil_plane(x)
-        return t[0] + a, t[1] + b
-
-    zero = (jnp.zeros((2 * kdim, kdim), F32), jnp.zeros((kdim, kdim), F32))
+
+    def products(x, b):
+        at = pl.ds(pl.multiple_of(b * 2 * cz, 2 * cz), 2 * cz)
+        hacc[...] += lax.dot_general(
+            sb[x, :, at], ab[x, 0:kdim, at], NT, preferred_element_type=F32
+        )
+        hlow[...] += lax.dot_general(
+            sb[x, 0:kdim, at], ab[x, kdim : 2 * kdim, at], NT, preferred_element_type=F32
+        )
+
+    def all_products(x):
+        for b in range(cy // 2):
+            products(x, b)
+
+    def stencil_next(x, c):
+        stencil_plane(x, x - 1)
+        return c
+
+    hacc[...] = jnp.zeros(hacc.shape, F32)
+    hlow[...] = jnp.zeros(hlow.shape, F32)
     half = cx // 2
-    t = lax.fori_loop(1, half, stencil_sum, zero)
+    stencil_plane(1, None)
+    lax.fori_loop(2, half, stencil_next, 0)
     gram.spread()
-    t = lax.fori_loop(half, cx - 1, stencil_sum, t)
+    lax.fori_loop(half, cx - 1, stencil_next, 0)
 
     @pl.when(me > 0)
     def _():
@@ -255,7 +284,7 @@
     def _():
         s2[0] = jnp.zeros(s2.shape[1:], F32)
 
-    t = stencil_sum(0, t)
+    stencil_plane(0, cx - 2)
 
     @pl.when(me < n - 1)
     def _():
@@ -265,18 +294,26 @@
     def _():
         s2[cx + 1] = jnp.zeros(s2.shape[1:], F32)
 
-    t = stencil_sum(cx - 1, t)
-    ht[...] = (t[0][:kdim] + t[0][kdim:] + t[1]).reshape(ht.shape)
+    stencil_plane(cx - 1, 0)
+    all_products(cx - 1)
+    ht[...] = (hacc[:kdim] + hacc[kdim:] + hlow[...]).reshape(ht.shape)
     hess.scatter()
 
     gram.finish()
     ncells = cx * n * cy * cz
-    rest = gtot[...].reshape(kdim, kdim) * (1.0 / ncells)
+    full = gtot[...].reshape(kdim, kdim) * (1.0 / ncells)
+    rows, cols = (lax.broadcasted_iota(jnp.int32, (kdim, kdim), d) for d in (0, 1))
+    on_diagonal = jnp.where(rows == cols, full, 0.0)
+    norm = jnp.sqrt(jnp.sum(on_diagonal, axis=0, keepdims=True))
+    inv_norm = 1.0 / norm
+    rest = full * inv_norm * (1.0 / jnp.sqrt(jnp.sum(on_diagonal, axis=1, keepdims=True)))
     panels = kdim // 8
     done, rest = eliminate(rest, panels // 2, 0)
     hess.spread()
     more, rest = eliminate(rest, panels - panels // 2, panels // 2)
-    packed[...] = jnp.concatenate(done + more, axis=0)
+    rest = jnp.concatenate(done + more, axis=0)
+    pivots = jnp.sum(jnp.where(rows == cols, rest, 0.0), axis=1, keepdims=True)
+    packed[...] = rest * (1.0 / jnp.sqrt(pivots)) * jnp.where(cols >= rows, norm, inv_norm)
     hess.finish()
     hsum[...] = htot[...].reshape(kdim, kdim) * (1.0 / ncells)
 
@@ -305,9 +342,8 @@
     row = lax.broadcasted_iota(jnp.int32, (kdim, kdim), 0)
     col = lax.broadcasted_iota(jnp.int32, (kdim, kdim), 1)
     pivots = jnp.sum(jnp.where(row == col, a, 0.0), axis=1, keepdims=True)
-    scale = 1.0 / jnp.sqrt(pivots)
-    factor[...] = jnp.where(col >= row, a * scale, 0.0)
-    inverse = jnp.where(col < row, a, jnp.where(row == col, 1.0, 0.0)) * scale
+    factor[...] = jnp.where(col >= row, a, 0.0)
+    inverse = jnp.where(col < row, a, jnp.where(row == col, 1.0 / pivots, 0.0))
     high, low = parts_of(inverse)
     twice = jnp.concatenate([high, high], axis=1)
 
@@ -364,6 +400,8 @@
             pltpu.VMEM((cx + 2, cy, kdim, cz), F32),
             pltpu.VMEM((cx, 2 * kdim, cy * cz), BF16),
             pltpu.VMEM((cx, 2 * kdim, cy * cz), BF16),
+            pltpu.VMEM((2 * kdim, kdim), F32),
+            pltpu.VMEM((kdim, kdim), F32),
             *summed,
             *summed,
             dma((cx, cy)), dma((2,)), dma((2,)), dma((cx,)),

time: 53.5 us -> 51.5 us (0.963)
  Pallas kernels: 51.9 us -> 49.9 us
    pallas_call x1, Pallas kernels: 45 us -> 43 us  [shards(): pl.pallas_call(functools.partial(reduce_kernel, n, owners), out_shape=(sq...]
where the time goes in v2:
time: 51.5 us; the launch traced here: 51.3 us
  Pallas kernels  49.9 us (97%)
  local copies, waits for them, and re-layouts  0.79 us (2%)
  between operations  0.65 us (1%)
    pallas_call x1, Pallas kernels, shards(): pl.pallas_call(functools.partial(reduce_kernel, n, owners), out_shape=(sq...  43 us
    pallas_call x1, Pallas kernels, shards(): pl.pallas_call(image_kernel, out_shape=(square, jax.ShapeDtypeStruct((kdi...  6.92 us

profile of v2, /device:TPU:0, one launch (start us, length us, event | category | flops | bytes accessed | tf_op | source)
XLA Modules:
  0.0 51.3 jit_solution(7742755646871148712)
XLA Ops:
  0.6 0.0 copy-start
  0.6 0.8 %copy-done = f32[12,8,128]{2,1,0:T(8,128)S(1)} copy-done((f32[12,8,128]{2,1,0:T(8,128)S(1)}, f32[12,8,128]{2,1,0:T(8,128)}, u32[]{:S(2)}) %copy-start) | copy-done | bytes 49176
  1.4 43.0 %reduce_kernel.1 = (f32[128,128]{1,0:T(8,128)S(1)}, f32[128,128]{1,0:T(8,128)S(1)}, bf16[12,256,1024]{2,1,0:T(8,128)(2,1)}) custom-call(f32[128,96,1,128]{3,2,1,0:T(1,128)} %bitcast.2, f32[12,8,128]{2,1,0:T(8,128)S(1)} %copy-done), custom_call_target="tpu_custom_call" | custom-call | tf_op jit(solution)/shard_map/reduce_kernel/pallas_call | solution.py:394
  44.4 6.9 %image_kernel.1 = (f32[128,128]{1,0:T(8,128)}, f32[128,96,1,128]{3,2,1,0:T(1,128)}, f32[128,128]{1,0:T(8,128)}) custom-call(f32[128,128]{1,0:T(8,128)S(1)} %get-tuple-element.9.packed, f32[128,128]{1,0:T(8,128)S(1)} %get-tuple-element.10.hsum, bf16[12,256,1024]{2,1,0:T(8,128)(2,1)} %get-tuple-element.11.applied), custom_call_target="tpu_custom_call" | custom-call | tf_op jit(solution)/shard_map/image_kernel/pallas_call | solution.py:416
Async XLA Ops:
  0.6 0.8 %copy-start = (f32[12,8,128]{2,1,0:T(8,128)S(1)}, f32[12,8,128]{2,1,0:T(8,128)}, u32[]{:S(2)}) copy-start(f32[12,8,128]{2,1,0:T(8,128)} %coef.1) | copy-start | bytes 147460

commit v3 on v2

--- a/solution.py
+++ b/solution.py
@@ -150,8 +150,8 @@
 
 
 def reduce_kernel(
-    n, owners, snap, coef, packed, hsum, applied,
-    s2, sb, ab, hacc, hlow, gt, gs, gtot, ht, hs, htot,
+    n, owners, snap, coef_in, packed, hsum, applied,
+    coef, coef_sem, s2, sb, ab, hacc, hlow, gt, gs, gtot, ht, hs, htot,
     load_sem, halo_send, halo_recv, out_sem,
     g0, g1, g2, g3, h0, h1, h2, h3,
 ):
@@ -181,6 +181,8 @@
         return c
 
     lax.fori_loop(0, cx, load_plane, 0)
+    coefficients = pltpu.make_async_copy(coef_in, coef, coef_sem)
+    coefficients.start()
     pl.semaphore_wait(barrier, n - 1)
 
     to_right = pltpu.make_async_remote_copy(
@@ -206,10 +208,11 @@
         return lax.dot_general(sb[x], sb[x, 0:kdim], NT, preferred_element_type=F32)
 
     total = gram_plane(cx - 1) + gram_plane(0)
-    total = lax.fori_loop(1, cx - 1, lambda x, t: t + gram_plane(x), total)
+    total = lax.fori_loop(1, cx - 1, lambda x, t: t + gram_plane(x), total, unroll=2)
     cross = total[kdim:]
     gt[...] = (total[:kdim] + (cross + cross.T)).reshape(gt.shape)
     gram.scatter()
+    coefficients.wait()
 
     lane = lax.broadcasted_iota(jnp.int32, (1, 1, cz), 2)
     from_low = jnp.where(lane == 0, 0.0, 0.5)
@@ -365,7 +368,7 @@
             store(x, y + 1).start()
         return c
 
-    lax.fori_loop(0, cx, plane, 0)
+    lax.fori_loop(0, cx, plane, 0, unroll=2)
     left = jnp.dot(inverse, hsum[...], precision=HIGH, preferred_element_type=F32)
     reduced[...] = lax.dot_general(left, inverse, NT, precision=HIGH, preferred_element_type=F32)
 
@@ -394,9 +397,11 @@
     packed, hsum, applied = pl.pallas_call(
         functools.partial(reduce_kernel, n, owners),
         out_shape=(square, square, jax.ShapeDtypeStruct((cx, 2 * kdim, cy * cz), BF16)),
-        in_specs=[hbm, vmem],
+        in_specs=[hbm, hbm],
         out_specs=(vmem, vmem, hbm),
         scratch_shapes=[
+            pltpu.VMEM((cx, cy, cz), F32),
+            dma,
             pltpu.VMEM((cx + 2, cy, kdim, cz), F32),
             pltpu.VMEM((cx, 2 * kdim, cy * cz), BF16),
             pltpu.VMEM((cx, 2 * kdim, cy * cz), BF16),

time: 51.5 us -> 51.5 us (level)
  no operation moved by 1% of the time
where the time goes in v3:
time: 51.5 us; the launch traced here: 51.3 us
  Pallas kernels  49.9 us (97%)
  local copies, waits for them, and re-layouts  0.79 us (2%)
  between operations  0.65 us (1%)
    pallas_call x1, Pallas kernels, shards(): pl.pallas_call(functools.partial(reduce_kernel, n, owners), out_shape=(sq...  43 us
    pallas_call x1, Pallas kernels, shards(): pl.pallas_call(image_kernel, out_shape=(square, jax.ShapeDtypeStruct((kdi...  6.93 us

profile of v3, /device:TPU:0, one launch (start us, length us, event | category | flops | bytes accessed | tf_op | source)
XLA Modules:
  0.0 51.3 jit_solution(11266158304052647128)
XLA Ops:
  0.6 0.0 copy-start
  0.6 0.8 %copy-done = f32[12,8,128]{2,1,0:T(8,128)S(1)} copy-done((f32[12,8,128]{2,1,0:T(8,128)S(1)}, f32[12,8,128]{2,1,0:T(8,128)}, u32[]{:S(2)}) %copy-start) | copy-done | bytes 49176
  1.4 43.0 %reduce_kernel.1 = (f32[128,128]{1,0:T(8,128)S(1)}, f32[128,128]{1,0:T(8,128)S(1)}, bf16[12,256,1024]{2,1,0:T(8,128)(2,1)}) custom-call(f32[128,96,1,128]{3,2,1,0:T(1,128)} %bitcast.2, f32[12,8,128]{2,1,0:T(8,128)S(1)} %copy-done), custom_call_target="tpu_custom_call" | custom-call | tf_op jit(solution)/shard_map/reduce_kernel/pallas_call | solution.py:397
  44.4 6.9 %image_kernel.1 = (f32[128,128]{1,0:T(8,128)}, f32[128,96,1,128]{3,2,1,0:T(1,128)}, f32[128,128]{1,0:T(8,128)}) custom-call(f32[128,128]{1,0:T(8,128)S(1)} %get-tuple-element.9.packed, f32[128,128]{1,0:T(8,128)S(1)} %get-tuple-element.10.hsum, bf16[12,256,1024]{2,1,0:T(8,128)(2,1)} %get-tuple-element.11.applied), custom_call_target="tpu_custom_call" | custom-call | tf_op jit(solution)/shard_map/image_kernel/pallas_call | solution.py:421
Async XLA Ops:
  0.6 0.8 %copy-start = (f32[12,8,128]{2,1,0:T(8,128)S(1)}, f32[12,8,128]{2,1,0:T(8,128)}, u32[]{:S(2)}) copy-start(f32[12,8,128]{2,1,0:T(8,128)} %coef_in.1) | copy-start | bytes 147460
